TPU v7x, 256 devices: a whole 4x4x8 slice. The times are simulated.
256 devices in a mesh: grp: 64 (over z_lo, x, y), sp: 4 (over z_hi, core).
Axes of the slice: x: 4, y: 4, z: 8 (z_hi: 2, z_lo: 4; z = z_hi * 4 + z_lo), core: 2. Of those that a mesh axis runs over, the one named last changes fastest.
Arguments:
- queries: bfloat16 [32768, 2048], P(('grp', 'sp')), may hold values from -6 to 6
- keys: bfloat16 [32768, 1024], P(('grp', 'sp')), may hold values from -6 to 6
- values: bfloat16 [32768, 1024], P(('grp', 'sp')), may hold values from -6 to 6
- doc_ids: int32 [32768], P(('grp', 'sp')), may hold values from 0 to 127, as said below
- w_out: bfloat16 [2048, 4608], P('sp', 'grp'), may hold values from -0.125 to 0.125
- cotangent: bfloat16 [32768, 4608], P(('grp', 'sp')), may hold values from -24 to 24
Outputs:
- mixed: bfloat16 [32768, 4608], P(('grp', 'sp'))
- query_grad: bfloat16 [32768, 2048], P(('grp', 'sp'))
- key_grad: bfloat16 [32768, 1024], P(('grp', 'sp'))
- value_grad: bfloat16 [32768, 1024], P(('grp', 'sp'))
- w_grad: float32 [2048, 4608], P('sp', 'grp')
Inputs may be any that keep to these rules, and one draw needn't show every extreme that they name: `doc_ids`: each group of 512 consecutive tokens holds one or two whole documents; document numbers never fall along the tokens; every document holds 128 to 512 tokens, and some document holds exactly 512.
All inputs are finite; a program needn't handle non-finite values.
Results may differ from a plain program's by a relative error of at most 0.017.
Values may be sent and summed in bfloat16 or wider, within the bound.
No kernel may reach another device: no remote copies, remote signals or barrier semaphores. Data moves between devices by JAX's collectives and lax.ppermute only.
A program may use at most 128 MiB of HBM per device.

v0:
```python
import jax
import jax.numpy as jnp
from jax import lax
from jax.sharding import PartitionSpec as P

HD = 128


query_scale = 1.0 / 12.0
softcap = 50.0


def attend(q_heads, k_heads, v_heads, seg_rows, grad_heads):
    length = q_heads.shape[0]
    kv_local = k_heads.shape[1] // HD
    repeat = q_heads.shape[1] // HD // kv_local
    queries4 = q_heads.reshape(length, kv_local, repeat, HD)
    keys3 = k_heads.reshape(length, kv_local, HD)
    values3 = v_heads.reshape(length, kv_local, HD)
    grads4 = grad_heads.reshape(length, kv_local, repeat, HD)
    query_block = min(512, length)
    key_tile_rows = min(128, length)
    query_count = length // query_block
    key_count = length // key_tile_rows

    def block_terms(query_rows, query_pos, query_seg, key_first_row):
        key_part = lax.dynamic_slice_in_dim(keys3, key_first_row, key_tile_rows, 0)
        key_seg = lax.dynamic_slice_in_dim(seg_rows, key_first_row, key_tile_rows, 0)
        key_pos = key_first_row + jnp.arange(key_tile_rows, dtype=jnp.int32)
        raw_scores = (
            jnp.einsum("qgrd,kgd->grqk", query_rows, key_part, preferred_element_type=jnp.float32)
            * query_scale
        )
        capped = softcap * jnp.tanh(raw_scores / softcap)
        visible = (query_seg[:, None] == key_seg[None, :]) & (
            query_pos[:, None] >= key_pos[None, :]
        )
        return (capped, jnp.where(visible, jnp.exp(capped), jnp.float32(0.0)))

    def per_query(carried, qindex):
        key_grad, value_grad = carried
        query_start = qindex * query_block
        query_pos = query_start + jnp.arange(query_block, dtype=jnp.int32)
        row_zeros = jnp.zeros((kv_local, repeat, query_block), jnp.float32)
        out_zeros = jnp.zeros((query_block, kv_local, repeat, HD), jnp.float32)

        def accumulate_running(key_index, output_totals):
            key_first_row = key_index * key_tile_rows

            def compute():
                return jnp.sum(
                    block_terms(queries4, query_pos, seg_rows, key_first_row)[1], axis=-1
                )

            return output_totals + compute()

        output_totals = lax.fori_loop(0, key_count, accumulate_running, row_zeros)

        def accumulate_output(key_index, running_total):
            key_first_row = key_index * key_tile_rows

            def compute():
                weights = block_terms(queries4, query_pos, seg_rows, key_first_row)[1]
                rounded = (weights / output_totals[..., None]).astype(jnp.bfloat16)
                value_part = lax.dynamic_slice_in_dim(values3, key_first_row, key_tile_rows, 0)
                return jnp.einsum(
                    "grqk,kgd->qgrd", rounded, value_part, preferred_element_type=jnp.float32
                )

            return running_total + compute()

        attended = lax.fori_loop(0, key_count, accumulate_output, out_zeros).astype(jnp.bfloat16)
        row_dots = jnp.einsum(
            "qgrd,qgrd->grq", grads4, attended, preferred_element_type=jnp.float32
        )

        def accumulate_gradients(key_index, carry_state):
            query_accum, key_accum, value_accum = carry_state
            key_first_row = key_index * key_tile_rows

            def compute():
                capped, weights = block_terms(queries4, query_pos, seg_rows, key_first_row)
                probability = weights / output_totals[..., None]
                rounded = probability.astype(jnp.bfloat16)
                key_part = lax.dynamic_slice_in_dim(keys3, key_first_row, key_tile_rows, 0)
                value_part = lax.dynamic_slice_in_dim(values3, key_first_row, key_tile_rows, 0)
                prob_grad = jnp.einsum(
                    "qgrd,kgd->grqk", grads4, value_part, preferred_element_type=jnp.float32
                )
                score_grad = (
                    probability
                    * (prob_grad - row_dots[..., None])
                    * (1.0 - (capped / softcap) ** 2)
                ).astype(jnp.bfloat16)
                return (
                    jnp.einsum(
                        "grqk,kgd->qgrd", score_grad, key_part, preferred_element_type=jnp.float32
                    ),
                    jnp.einsum(
                        "grqk,qgrd->kgd", score_grad, queries4, preferred_element_type=jnp.float32
                    ),
                    jnp.einsum(
                        "grqk,qgrd->kgd", rounded, grads4, preferred_element_type=jnp.float32
                    ),
                )

            query_term, key_term, value_term = compute()
            key_accum = lax.dynamic_update_slice_in_dim(
                key_accum,
                lax.dynamic_slice_in_dim(key_accum, key_first_row, key_tile_rows, 0) + key_term,
                key_first_row,
                0,
            )
            value_accum = lax.dynamic_update_slice_in_dim(
                value_accum,
                lax.dynamic_slice_in_dim(value_accum, key_first_row, key_tile_rows, 0) + value_term,
                key_first_row,
                0,
            )
            return (query_accum + query_term, key_accum, value_accum)

        query_grad, key_grad, value_grad = lax.fori_loop(
            0, key_count, accumulate_gradients, (out_zeros, key_grad, value_grad)
        )
        query_grad = (query_grad * query_scale).astype(jnp.bfloat16)
        return ((key_grad, value_grad), (attended, query_grad))

    kv_start = jnp.zeros((length, kv_local, HD), jnp.float32)
    (key_grad, value_grad), (attended, query_grad) = lax.scan(
        per_query, (kv_start, kv_start), jnp.arange(query_count, dtype=jnp.int32)
    )
    attended = attended.reshape(length, kv_local * repeat * HD)
    query_grad = query_grad.reshape(length, kv_local * repeat * HD)
    key_grad = (key_grad * query_scale).astype(jnp.bfloat16).reshape(length, kv_local * HD)
    value_grad = value_grad.astype(jnp.bfloat16).reshape(length, kv_local * HD)
    return (attended, query_grad, key_grad, value_grad)


def local(queries, keys, values, doc_ids, w_out, cotangent):
    q_heads, k_heads, v_heads = (
        lax.all_to_all(queries, "sp", split_axis=1, concat_axis=0, tiled=True),
        lax.all_to_all(keys, "sp", split_axis=1, concat_axis=0, tiled=True),
        lax.all_to_all(values, "sp", split_axis=1, concat_axis=0, tiled=True),
    )
    cot_rows, seg_rows = (
        lax.all_gather(cotangent, "sp", axis=0, tiled=True),
        lax.all_gather(doc_ids, "sp", axis=0, tiled=True),
    )
    contract_last = (((1,), (1,)), ((), ()))
    columns = cot_rows
    grad_heads = lax.dot_general(
        columns,
        lax.all_gather(w_out, "grp", axis=1, tiled=True),
        contract_last,
        preferred_element_type=jnp.float32,
    ).astype(jnp.bfloat16)
    attended, query_grad, key_grad, value_grad = attend(
        q_heads, k_heads, v_heads, seg_rows, grad_heads
    )
    partial_out = jnp.dot(
        attended,
        lax.all_gather(w_out, "grp", axis=1, tiled=True),
        preferred_element_type=jnp.float32,
    )
    mixed = lax.psum_scatter(partial_out, "sp", scatter_dimension=0, tiled=True).astype(
        jnp.bfloat16
    )
    columns = cot_rows
    w_grad = lax.psum_scatter(
        lax.dot_general(
            columns, attended, (((0,), (0,)), ((), ())), preferred_element_type=jnp.float32
        ),
        "grp",
        scatter_dimension=0,
        tiled=True,
    ).T
    query_back, key_back, value_back = (
        lax.all_to_all(query_grad, "sp", split_axis=0, concat_axis=1, tiled=True),
        lax.all_to_all(key_grad, "sp", split_axis=0, concat_axis=1, tiled=True),
        lax.all_to_all(value_grad, "sp", split_axis=0, concat_axis=1, tiled=True),
    )
    return (mixed, query_back, key_back, value_back, w_grad)


def solution(mesh):
    return jax.shard_map(
        local,
        mesh=mesh,
        in_specs=(
            P(("grp", "sp"), None),
            P(("grp", "sp"), None),
            P(("grp", "sp"), None),
            P(("grp", "sp")),
            P("sp", "grp"),
            P(("grp", "sp"), None),
        ),
        out_specs=(
            P(("grp", "sp"), None),
            P(("grp", "sp"), None),
            P(("grp", "sp"), None),
            P(("grp", "sp"), None),
            P("sp", "grp"),
        ),
        check_vma=False,
    )
```

profile of v0, /device:TPU:0, one launch (start us, length us, event | category | flops | bytes accessed | tf_op | source)
XLA Modules:
  0.0 1024.6 jit_solution(14348743522527731142)
XLA Ops:
  7.2 0.7 all-gather.6.cloned.1.call-update
  8.0 0.7 all-gather.4.cloned.1.call-update
  8.7 1.7 copy.141
  10.3 6.7 all-to-all-start
  17.1 1.7 copy.140
  18.7 8.4 all-to-all-done
  27.1 3.4 all-to-all-start.1
  30.5 1.9 copy.139
  32.4 26.0 %all-to-all-done.1 = bf16[128,4,256]{2,0,1:T(8,128)(2,1)S(1)} async-done(((bf16[128,4,256]{2,0,1:T(8,128)(2,1)}), bf16[128,4,256]{2,0,1:T(8,128)(2,1)S(1)}, u32[]{:S(2)}, u32[]{:S(2)}) %all-to-all-start.1) | async-done | bytes 262176 | tf_op jit(solution)/shard_map/all_to_all | solution.py:142
  58.4 3.5 all-to-all-start.2
  62.0 25.9 %all-gather = s32[4,1,128]{2,1,0:T(1,128)S(1)} all-gather(s32[1,1,128]{2,1,0:T(1,128)S(1)} %bitcast.211), channel_id=1, replica_groups=mesh['grp'=64,'sp'=4] {'sp'}, dimensions={0}, use_global_device_ids=true | all-gather | bytes 2560 | tf_op jit(solution)/shard_map/all_gather | solution.py:147
  88.3 3.1 while.70
  88.5 0.5 fusion.109
  89.3 0.5 fusion.109
  90.1 0.5 fusion.109
  90.9 0.5 fusion.109
  91.4 5.2 while.71
  91.8 0.9 fusion.114
  93.1 0.9 fusion.114
  94.4 0.9 fusion.114
  95.7 0.9 fusion.114
  96.6 3.4 all-gather.6.cloned.1.call-done
  100.0 354.8 %all-gather.4.cloned.1.call-done = bf16[512,4608]{0,1:T(8,128)(2,1)} async-done(((bf16[512,72]{0,1:T(8,128)(2,1)}), bf16[512,4608]{0,1:T(8,128)(2,1)}) %all-gather.4.cloned.1.call-update) | async-done | bytes 4718608 | tf_op jit(solution)/shard_map/all_gather | solution.py:153
  454.9 6.8 fusion.66
  461.7 5.1 fusion.67
  466.9 7.4 convolution_bitcast_fusion.5
  474.3 10.4 %copy.126 = f32[4608,512]{1,0:T(8,128)} copy(f32[4608,512]{0,1:T(8,128)} %convolution_bitcast_fusion.5) | data formatting | bytes 18874368
  484.7 1.0 copy.95
  485.7 0.8 broadcast_in_dim.115
  486.6 0.8 broadcast_in_dim.115.clone
  487.4 27.0 %while.72 = (s32[]{:T(128)}, f32[512,2,2,128]{0,3,2,1:T(8,128)S(1)}, f32[512,2,128]{2,0,1:T(8,128)}, f32[512,2,128]{2,0,1:T(8,128)}, bf16[512,2,128]{2,0,1:T(8,1...) while((s32[]{:T(128)}, ...), condition=%wide.region_7.8_spmd.clone, body=%wide.region_6.7_spmd.clone.sunk | while | flops 340000896 | bytes 12088097 | solution.py:122
  488.1 1.6 fusion.126
  489.7 0.4 fusion.127
  490.1 1.9 fusion.128
  492.0 2.1 fusion.129
  494.9 1.5 fusion.126
  496.4 0.4 fusion.127
  496.9 1.9 fusion.128
  498.7 2.1 fusion.129
  501.6 1.6 fusion.126
  503.2 0.4 fusion.127
  503.6 1.9 fusion.128
  505.5 2.1 fusion.129
  508.4 1.5 fusion.126
  509.9 0.4 fusion.127
  510.4 1.9 fusion.128
  512.2 2.1 fusion.129
  514.4 1.1 multiply_convert_fusion.1
  515.8 0.9 all_to_all.91
  516.6 4.6 all-to-all-start.4
  521.3 1.1 convert_element_type.55
  522.6 0.9 all_to_all.95
  523.5 16.8 %all-to-all-done.4 = bf16[4,128,256]{2,1,0:T(8,128)(2,1)S(1)} async-done(((bf16[4,128,256]{2,1,0:T(8,128)(2,1)}), bf16[4,128,256]{2,1,0:T(8,128)(2,1)S(1)}, u32[]{:S(2)}, u32[]{:S(2)}) %all-to-all-start.4) | async-done | bytes 262176 | tf_op jit(solution)/shard_map/all_to_all | solution.py:179
  540.3 3.4 all-to-all-start.5
  544.0 1.1 copy.123
  545.1 21.7 %all-to-all-done.5 = bf16[4,128,256]{2,1,0:T(8,128)(2,1)S(1)} async-done(((bf16[4,128,256]{2,1,0:T(8,128)(2,1)}), bf16[4,128,256]{2,1,0:T(8,128)(2,1)S(1)}, u32[]{:S(2)}, u32[]{:S(2)}) %all-to-all-start.5) | async-done | bytes 262176 | tf_op jit(solution)/shard_map/all_to_all | solution.py:180
  566.8 3.5 all-to-all-start.3
  570.4 0.9 copy.103
  571.4 0.9 copy.104
  572.3 33.4 %all-to-all-done.3 = bf16[4,128,512]{2,1,0:T(8,128)(2,1)S(1)} async-done(((bf16[4,128,512]{2,1,0:T(8,128)(2,1)}), bf16[4,128,512]{2,1,0:T(8,128)(2,1)S(1)}, u32[]{:S(2)}, u32[]{:S(2)}) %all-to-all-start.3) | async-done | bytes 524320 | tf_op jit(solution)/shard_map/all_to_all | solution.py:178
  606.0 1.0 copy.102
  607.0 18.0 %reduce-scatter.5.cloned.1.call-done = f32[128,4608]{1,0:T(8,128)} async-done(((f32[512,4608]{1,0:T(8,128)}), f32[128,4608]{1,0:T(8,128)}) %reduce-scatter.5.cloned.1.call-update) | async-done | bytes 2359312 | tf_op jit(solution)/shard_map/reduce_scatter | solution.py:165
  625.0 2.8 convert_element_type.51
  627.8 390.3 %reduce-scatter.7.cloned.1.call-done = f32[72,512]{1,0:T(8,128)} async-done(((f32[4608,512]{1,0:T(8,128)}), f32[72,512]{1,0:T(8,128)}) %reduce-scatter.7.cloned.1.call-update) | async-done | bytes 147472
  (100 shorter events, 7.3 us)
Async XLA Ops:
  7.2 54.8 %copy-start.3 = (s32[128]{0:T(128)S(1)}, s32[128]{0:T(128)}, u32[]{:S(2)}) copy-start(s32[128]{0:T(128)} %param.15) | copy-start | bytes 1540
  7.2 92.9 %all-gather.6.cloned.1.call-start = ((), (), s32[]{:S(2)}) async-start(), calls=%async_computation.10 | async-start | bytes 5898240 | tf_op jit(solution)/shard_map/all_gather | solution.py:146
  7.9 447.0 %all-gather.4.cloned.1.call-start = ((), (), s32[]{:S(2)}) async-start(), calls=%async_computation.8 | async-start | bytes 4792320 | tf_op jit(solution)/shard_map/all_gather | solution.py:153
  10.3 16.8 %all-to-all-start = ((bf16[128,4,256]{2,0,1:T(8,128)(2,1)}), bf16[128,4,256]{2,0,1:T(8,128)(2,1)S(1)}, u32[]{:S(2)}, u32[]{:S(2)}) async-start(bf16[128,4,256]{2,0,1:T(8,128)(2,1)} %bitcast.147), calls=%async_computation | async-start | bytes 524288 | tf_op jit(solution)/shard_map/all_to_all | solution.py:143
  27.1 31.3 %all-to-all-start.1 = ((bf16[128,4,256]{2,0,1:T(8,128)(2,1)}), bf16[128,4,256]{2,0,1:T(8,128)(2,1)S(1)}, u32[]{:S(2)}, u32[]{:S(2)}) async-start(bf16[128,4,256]{2,0,1:T(8,128)(2,1)} %bitcast.146), calls=%async_computation.1 | async-start | bytes 524288 | tf_op jit(solution)/shard_map/all_to_all | solution.py:142
  58.4 29.7 %all-to-all-start.2 = ((bf16[128,4,512]{2,0,1:T(8,128)(2,1)}), bf16[128,4,512]{2,0,1:T(8,128)(2,1)S(1)}, u32[]{:S(2)}, u32[]{:S(2)}) async-start(bf16[128,4,512]{2,0,1:T(8,128)(2,1)} %bitcast.145), calls=%async_computation.2 | async-start | bytes 1048576 | tf_op jit(solution)/shard_map/all_to_all | solution.py:141
  61.9 563.1 %reduce-scatter.5.cloned.1.call-start = ((), (), s32[]{:S(2)}) async-start(), calls=%async_computation.9 | async-start | bytes 11796480 | tf_op jit(solution)/shard_map/reduce_scatter | solution.py:165
  96.6 358.3 %copy-start.4 = (f32[512,2,2,128]{0,3,2,1:T(8,128)}, f32[512,2,2,128]{0,3,2,1:T(8,128)S(1)}, u32[]{:S(2)}) copy-start(f32[512,2,2,128]{0,3,2,1:T(8,128)S(1)} %get-tuple-element.709) | copy-start | bytes 3145732
  454.9 6.8 copy-start
  466.8 551.3 %reduce-scatter.7.cloned.1.call-start = ((), (), s32[]{:S(2)}) async-start(), calls=%async_computation.11 | async-start | bytes 9584640
  487.4 0.7 copy-start.1
  492.0 2.1 copy-start.2
  494.1 0.7 copy-start.1
  498.7 2.1 copy-start.2
  500.9 0.7 copy-start.1
  505.5 2.1 copy-start.2
  507.6 0.7 copy-start.1
  512.2 2.1 copy-start.2
  516.6 23.7 %all-to-all-start.4 = ((bf16[4,128,256]{2,1,0:T(8,128)(2,1)}), bf16[4,128,256]{2,1,0:T(8,128)(2,1)S(1)}, u32[]{:S(2)}, u32[]{:S(2)}) async-start(bf16[4,128,256]{2,1,0:T(8,128)(2,1)} %all_to_all.91), calls=%async_computation.5 | async-start | bytes 524288 | tf_op jit(solution)/shard_map/all_to_all | solution.py:179
  540.3 26.5 %all-to-all-start.5 = ((bf16[4,128,256]{2,1,0:T(8,128)(2,1)}), bf16[4,128,256]{2,1,0:T(8,128)(2,1)S(1)}, u32[]{:S(2)}, u32[]{:S(2)}) async-start(bf16[4,128,256]{2,1,0:T(8,128)(2,1)} %all_to_all.95), calls=%async_computation.6 | async-start | bytes 524288 | tf_op jit(solution)/shard_map/all_to_all | solution.py:180
  566.8 39.0 %all-to-all-start.3 = ((bf16[4,128,512]{2,1,0:T(8,128)(2,1)}), bf16[4,128,512]{2,1,0:T(8,128)(2,1)S(1)}, u32[]{:S(2)}, u32[]{:S(2)}) async-start(bf16[4,128,512]{2,1,0:T(8,128)(2,1)} %copy.123), calls=%async_computation.4 | async-start | bytes 1048576 | tf_op jit(solution)/shard_map/all_to_all | solution.py:178
Sparse Core Ops, SparseCore 0:
  9.8 90.1 all-gather.5
  101.8 353.0 all-gather.3
  466.9 158.0 reduce-scatter.4
  628.0 390.0 reduce-scatter.6
where the time goes:
time: 1030 us; the launch traced here: 1020 us
  waiting for transfers between devices  874 us (85%)
  matrix products  49.9 us (5%)
  local copies, waits for them, and re-layouts  28 us (3%)
  blocking collectives  25.9 us (3%)
  starting transfers between devices  25.3 us (2%)
  between operations  14 us (1%)
    unnamed x5, waiting for transfers between devices  392 us
    all_gather x1, waiting for transfers between devices, local(): lax.all_gather(w_out, 'grp', axis=1, tiled=True)  355 us
    all_to_all x1, waiting for transfers between devices, local(): lax.all_to_all(query_grad, 'sp', split_axis=0, concat_axis=1, tiled=True)  33.4 us
    all_to_all x1, waiting for transfers between devices, local(): lax.all_to_all(keys, 'sp', split_axis=1, concat_axis=0, tiled=True)  26 us
    all_gather x1, blocking collectives, local(): lax.all_gather(doc_ids, 'sp', axis=0, tiled=True)  25.9 us
    all_to_all x1, waiting for transfers between devices, local(): lax.all_to_all(value_grad, 'sp', split_axis=0, concat_axis=1, tiled=True)  21.7 us
  transfers between devices with their start and end apart: 10, of which 9 were waited for; matrix products, arithmetic and copies ran while one was open for 7% of the time, Pallas kernels for 0%

commit v1 on v0

v1 whole, which is shorter than its diff:
```python
import jax
import jax.numpy as jnp
from jax import lax
from jax.experimental import pallas as pl
from jax.experimental.pallas import tpu as pltpu
from jax.sharding import Mesh, PartitionSpec as P

HD = 128
SCALE = 1.0 / 12.0
CAP = 50.0
F32 = jnp.float32
BF16 = jnp.bfloat16
NT = (((1,), (1,)), ((), ()))
TN = (((0,), (0,)), ((), ()))
Z = ("zl", "zh")


def dot(a, b, dims=(((1,), (0,)), ((), ()))):
    return lax.dot_general(a, b, dims, preferred_element_type=F32)


def shift(a, axis, step):
    return lax.ppermute(a, axis, [(i, (i + step) % 4) for i in range(4)])


def z_index(z):
    z = z % 8
    return (z % 4) * 2 + z // 4


def shift_z(a, step):
    return lax.ppermute(a, Z, [(z_index(z), z_index(z + step)) for z in range(8)])


def swap_core(a):
    return lax.ppermute(a, "c", [(0, 1), (1, 0)])


def pick(a, index, axis):
    return lax.dynamic_index_in_dim(a, index, axis, keepdims=False)


def forward_kernel(q_ref, ko_ref, kx_ref, vo_ref, vx_ref, m_ref, att_ref, p_ref, d_ref):
    for r in range(2):
        cols = slice(r * HD, (r + 1) * HD)
        q = q_ref[:, cols]
        parts = []
        for half, k_ref in ((0, ko_ref), (1, kx_ref)):
            t = jnp.tanh(dot(q, k_ref[...], NT) * (SCALE / CAP))
            w = jnp.exp(CAP * t) * m_ref[:, half * 256 : half * 256 + 256]
            parts.append((t, w))
        total = sum(jnp.sum(w, axis=-1, keepdims=True) for _, w in parts)
        inverse = 1.0 / total
        att = 0.0
        for half, v_ref in ((0, vo_ref), (1, vx_ref)):
            t, w = parts[half]
            p = w * inverse
            rounded = p.astype(BF16)
            keys = slice(half * 256, half * 256 + 256)
            p_ref[r, :, keys] = rounded
            d_ref[r, :, keys] = p * (1.0 - t * t)
            att = att + dot(rounded, v_ref[...])
        att_ref[:, cols] = att.astype(BF16)


def backward_kernel(
    q_ref, ko_ref, kx_ref, vo_ref, vx_ref, att_ref, p_ref, d_ref, g_ref,
    dq_ref, dko_ref, dkx_ref, dvo_ref, dvx_ref,
):
    dk = [0.0, 0.0]
    dv = [0.0, 0.0]
    for r in range(2):
        cols = slice(r * HD, (r + 1) * HD)
        q = q_ref[:, cols]
        g = g_ref[:, cols]
        row = jnp.sum(g.astype(F32) * att_ref[:, cols].astype(F32), axis=-1, keepdims=True)
        dq = 0.0
        for half, k_ref, v_ref in ((0, ko_ref, vo_ref), (1, kx_ref, vx_ref)):
            keys = slice(half * 256, half * 256 + 256)
            dp = dot(g, v_ref[...], NT)
            ds = (d_ref[r, :, keys] * (dp - row)).astype(BF16)
            dq = dq + dot(ds, k_ref[...])
            dk[half] = dk[half] + dot(ds, q, TN)
            dv[half] = dv[half] + dot(p_ref[r, :, keys], g, TN)
        dq_ref[:, cols] = (dq * SCALE).astype(BF16)
    dko_ref[...] = dk[0] * SCALE
    dkx_ref[...] = (dk[1] * SCALE).astype(BF16)
    dvo_ref[...] = dv[0]
    dvx_ref[...] = dv[1].astype(BF16)


def pair_spec():
    return pl.BlockSpec((256, 2 * HD), lambda g: (0, g))


def key_spec():
    return pl.BlockSpec((256, HD), lambda g: (0, g))


def score_spec():
    return pl.BlockSpec((2, 256, 512), lambda g: (g, 0, 0))


def attend(q, ko, kx, vo, vx, mask):
    return pl.pallas_call(
        forward_kernel,
        grid=(4,),
        in_specs=[pair_spec(), key_spec(), key_spec(), key_spec(), key_spec(),
                  pl.BlockSpec((256, 512), lambda g: (0, 0))],
        out_specs=[pair_spec(), score_spec(), score_spec()],
        out_shape=[
            jax.ShapeDtypeStruct((256, 1024), BF16),
            jax.ShapeDtypeStruct((8, 256, 512), BF16),
            jax.ShapeDtypeStruct((8, 256, 512), F32),
        ],
        cost_estimate=pl.CostEstimate(
            flops=8 * 256 * 512 * 128 * 4, bytes_accessed=9 << 20, transcendentals=8 * 256 * 512 * 2
        ),
        compiler_params=pltpu.CompilerParams(vmem_limit_bytes=32 << 20),
        name="attend",
    )(q, ko, kx, vo, vx, mask)


def attend_back(q, ko, kx, vo, vx, att, p, d, g):
    return pl.pallas_call(
        backward_kernel,
        grid=(4,),
        in_specs=[pair_spec(), key_spec(), key_spec(), key_spec(), key_spec(),
                  pair_spec(), score_spec(), score_spec(), pair_spec()],
        out_specs=[pair_spec(), key_spec(), key_spec(), key_spec(), key_spec()],
        out_shape=[
            jax.ShapeDtypeStruct((256, 1024), BF16),
            jax.ShapeDtypeStruct((256, 512), F32),
            jax.ShapeDtypeStruct((256, 512), BF16),
            jax.ShapeDtypeStruct((256, 512), F32),
            jax.ShapeDtypeStruct((256, 512), BF16),
        ],
        cost_estimate=pl.CostEstimate(
            flops=8 * 256 * 512 * 128 * 8, bytes_accessed=11 << 20, transcendentals=0
        ),
        compiler_params=pltpu.CompilerParams(vmem_limit_bytes=32 << 20),
        name="attend_back",
    )(q, ko, kx, vo, vx, att, p, d, g)


def place(buffer, block, index, axis):
    return lax.dynamic_update_index_in_dim(buffer, block, index, axis)


def gather_axis(block, axis, at):
    me = lax.axis_index(axis)
    shape = block.shape[:at] + (4,) + block.shape[at:]
    out = place(jnp.zeros(shape, block.dtype), block, me, at)
    for step in (1, 3, 2):
        out = place(out, shift(block, axis, step), (me - step) % 4, at)
    return out


def gather_z(block):
    z = lax.axis_index("zh") * 4 + lax.axis_index("zl")

    def put(out, part, at):
        at = at % 8
        return lax.dynamic_update_slice(out, part[None, None], (at // 4, at % 4, 0, 0))

    out = put(jnp.zeros((2, 4) + block.shape, block.dtype), block, z)
    for step in (1, 7, 2, 6, 3, 5, 4):
        out = put(out, shift_z(block, step), z - step)
    return out


def scatter_axis(blocks, axis, at):
    me = lax.axis_index(axis)
    total = pick(blocks, me, at).astype(F32)
    for step in (1, 3, 2):
        total = total + shift(pick(blocks, (me + step) % 4, at), axis, step).astype(F32)
    return total.astype(BF16)


def scatter_z(first, second):
    blocks = jnp.stack([first, second])
    z = lax.axis_index("zh") * 4 + lax.axis_index("zl")

    def take(at):
        at = at % 8
        part = lax.dynamic_slice(blocks, (at // 4, at % 4, 0, 0), (1, 1) + blocks.shape[2:])
        return part.reshape(blocks.shape[2:])

    total = take(z).astype(F32)
    for step in (1, 7, 2, 6, 3, 5, 4):
        total = total + shift_z(take(z + step), step).astype(F32)
    return total


def local(queries, keys, values, doc_ids, w_out, cotangent):
    core = lax.axis_index("c")
    zh = lax.axis_index("zh")

    def by_core(a):
        a = a.reshape(128, 2, 2, a.shape[1] // 4)
        mine = pick(a, core, 2).reshape(128, -1)
        theirs = pick(a, 1 - core, 2).reshape(128, -1)
        return mine, theirs

    w_local = gather_z(w_out.T)
    w_first = gather_axis(gather_axis(w_local[0], "y", 1), "x", 1).reshape(4608, 512)
    w_second = gather_axis(gather_axis(w_local[1], "x", 1), "y", 2).reshape(4608, 512)

    q_mine, q_theirs = by_core(queries)
    k_mine, k_theirs = by_core(keys)
    v_mine, v_theirs = by_core(values)
    received = swap_core(jnp.concatenate([q_theirs, k_theirs, v_theirs], axis=1))
    q = jnp.concatenate([q_mine, received[:, :1024]], axis=0)
    kv = jnp.concatenate(
        [jnp.concatenate([k_mine, v_mine], axis=1), received[:, 1024:]], axis=0
    )
    cot = jnp.concatenate([cotangent, swap_core(cotangent)], axis=0)
    docs = jnp.concatenate([doc_ids, swap_core(doc_ids)]) + 1
    docs_before = lax.ppermute(docs, "zh", [(0, 1)])
    kv_before = lax.ppermute(kv, "zh", [(0, 1)])

    row = jnp.arange(128, dtype=jnp.int32)
    position = jnp.concatenate([core * 128 + row, (1 - core) * 128 + row])
    near = (docs[:, None] == docs[None, :]) & (position[:, None] >= position[None, :])
    far = docs[:, None] == docs_before[None, :]
    mask = jnp.concatenate([near, far], axis=1).astype(F32)

    ko, vo = kv[:, :512], kv[:, 512:]
    kx, vx = kv_before[:, :512], kv_before[:, 512:]
    att, probs, slopes = attend(q, ko, kx, vo, vx, mask)

    cot_t = cot.T
    g_first = dot(cot_t, att[:, :512]).astype(BF16).reshape(4, 4, 288, 512)
    g_second = dot(cot_t, att[:, 512:]).astype(BF16).reshape(4, 4, 4, 72, 512)
    g_first = scatter_axis(g_first, "x", 1).reshape(4, 4, 72, 512)
    g_second = scatter_axis(g_second, "y", 2)
    g_first = scatter_axis(g_first, "y", 1)
    g_second = scatter_axis(g_second, "x", 1)
    w_grad = scatter_z(g_first, g_second).T

    grads = jnp.concatenate([dot(cot, w_first), dot(cot, w_second)], axis=1).astype(BF16)
    dq, dko, dkx, dvo, dvx = attend_back(q, ko, kx, vo, vx, att, probs, slopes, grads)

    back = lax.ppermute(jnp.concatenate([dkx, dvx], axis=1), "zh", [(1, 0)])
    dkv = (jnp.concatenate([dko, dvo], axis=1) + back.astype(F32)).astype(BF16)

    partial = dot(att[:, :512], w_first, NT) + dot(att[:, 512:], w_second, NT)
    mixed = (partial[:128] + swap_core(partial[128:].astype(BF16)).astype(F32)).astype(BF16)

    def join(mine, theirs):
        mine = mine.reshape(128, 2, 1, -1)
        theirs = theirs.reshape(128, 2, 1, -1)
        low = jnp.where(core == 0, mine, theirs)
        high = jnp.where(core == 0, theirs, mine)
        return jnp.concatenate([low, high], axis=2).reshape(128, -1)

    dq_back = swap_core(dq[128:])
    dkv_back = swap_core(dkv[128:])
    return (
        mixed,
        join(dq[:128], dq_back),
        join(dkv[:128, :512], dkv_back[:, :512]),
        join(dkv[:128, 512:], dkv_back[:, 512:]),
        w_grad,
    )


def solution(mesh):
    fine = Mesh(mesh.devices.reshape(4, 4, 4, 2, 2), ("zl", "x", "y", "zh", "c"))
    tokens = ("zl", "x", "y", "zh", "c")
    rows = P(tokens, None)
    weight = P(("zh", "c"), ("zl", "x", "y"))
    return jax.shard_map(
        local,
        mesh=fine,
        in_specs=(rows, rows, rows, P(tokens), weight, rows),
        out_specs=(rows, rows, rows, rows, weight),
        check_vma=False,
    )
```

time: 1030 us -> 326 us (0.32)
  waiting for transfers between devices: 874 us -> 123 us
  starting transfers between devices: 25.3 us -> 101 us
  matrix products: 49.9 us -> 8.42 us
  local copies, waits for them, and re-layouts: 28 us -> 57.6 us
  blocking collectives: 25.9 us -> 0 us
  between operations: 14 us -> 2.6 us
  other arithmetic: 6.69 us -> 17.4 us
    unnamed x5 -> x0, waiting for transfers between devices: 392 us -> none
    all_gather x2 -> x0, waiting for transfers between devices: 358 us -> none  [the longest x1 355 us: local(): lax.all_gather(w_out, 'grp', axis=1, tiled=True)]
    ppermute x0 -> x47, waiting for transfers between devices: none -> 123 us  [the longest x24 90.7 us: shift(): return lax.ppermute(a, axis, [(i, (i + step) % 4) for i in range(4)])]
    all_to_all x6 -> x0, waiting for transfers between devices: 106 us -> none  [the longest x1 33.4 us: local(): lax.all_to_all(query_grad, 'sp', split_axis=0, concat_axis=1, tiled=True)]
    ppermute x0 -> x47, starting transfers between devices: none -> 101 us  [the longest x14 44.9 us: shift_z(): lax.ppermute(a, Z, [(z_index(z), z_index(z + step)) for z in range(8)])]
    dot_general x31 -> x6, matrix products: 49.9 us -> 8.42 us  [dot(): return lax.dot_general(a, b, dims, preferred_element_type=F32)]
    all_gather x1 -> x0, blocking collectives: 25.9 us -> none  [local(): lax.all_gather(doc_ids, 'sp', axis=0, tiled=True)]
    all_to_all x6 -> x0, starting transfers between devices: 25.1 us -> none  [the longest x1 6.72 us: local(): lax.all_to_all(values, 'sp', split_axis=1, concat_axis=0, tiled=True)]
  transfers between devices with their start and end apart: 10 -> 47, of which waited for: 9 -> 12; matrix products, arithmetic and copies ran while one was open for 7% -> 26% of each run, Pallas kernels for 0% -> 3%
where the time goes in v1:
time: 326 us; the launch traced here: 319 us
  waiting for transfers between devices  123 us (38%)
  starting transfers between devices  101 us (31%)
  local copies, waits for them, and re-layouts  57.6 us (18%)
  other arithmetic  17.4 us (5%)
  Pallas kernels  9.47 us (3%)
  matrix products  8.42 us (3%)
    ppermute x24, waiting for transfers between devices, shift(): return lax.ppermute(a, axis, [(i, (i + step) % 4) for i in range(4)])  90.7 us
    ppermute x14, starting transfers between devices, shift_z(): lax.ppermute(a, Z, [(z_index(z), z_index(z + step)) for z in range(8)])  44.9 us
    ppermute x24, starting transfers between devices, shift(): return lax.ppermute(a, axis, [(i, (i + step) % 4) for i in range(4)])  42.6 us
    dynamic_update_slice x16, local copies, waits for them, and re-layouts, place(): return lax.dynamic_update_index_in_dim(buffer, block, index, axis)  15.9 us
    ppermute x1, waiting for transfers between devices, local(): back = lax.ppermute(jnp.concatenate([dkx, dvx], axis=1), 'zh', [(1, 0)])  12.3 us
    dynamic_slice x6, local copies, waits for them, and re-layouts, pick(): return lax.dynamic_index_in_dim(a, index, axis, keepdims=False)  11 us
    ppermute x14, waiting for transfers between devices, shift_z(): lax.ppermute(a, Z, [(z_index(z), z_index(z + step)) for z in range(8)])  10.8 us
    dot_general x6, matrix products, dot(): return lax.dot_general(a, b, dims, preferred_element_type=F32)  8.42 us
  transfers between devices with their start and end apart: 47, of which 12 were waited for; matrix products, arithmetic and copies ran while one was open for 26% of the time, Pallas kernels for 3%

profile of v1, /device:TPU:0, one launch (start us, length us, event | category | flops | bytes accessed | tf_op | source)
XLA Modules:
  0.0 319.3 jit_solution(16678470951043467000)
XLA Ops:
  0.6 5.1 %collective-permute-start.9 = (bf16[72,512]{1,0:T(8,128)(2,1)}, bf16[72,512]{1,0:T(8,128)(2,1)}, u32[]{:S(2)}, u32[]{:S(2)}) collective-permute-start(bf16[72,512]{1,0:T(8,128)(2,1)} %bitcast.195), channel_id=1, source_target_pairs={{0,66},{64,130},{128,194},{192,0},{2,64},{66,128},{130,192},{194,2... | collective-permute-start | bytes 221192 | tf_op jit(solution)/shard_map/ppermute | solution.py:32
  5.7 4.6 %collective-permute-start.7 = (bf16[72,512]{1,0:T(8,128)(2,1)}, bf16[72,512]{1,0:T(8,128)(2,1)}, u32[]{:S(2)}, u32[]{:S(2)}) collective-permute-start(bf16[72,512]{1,0:T(8,128)(2,1)} %bitcast.197), channel_id=1, source_target_pairs={{0,130},{64,194},{128,0},{192,64},{2,128},{66,192},{130,2},{194,66... | collective-permute-start | bytes 221192 | tf_op jit(solution)/shard_map/ppermute | solution.py:32
  13.7 3.6 %dynamic-slice_reduce_fusion.2 = (bf16[128,2,256]{2,1,0:T(2,128)(2,1)S(1)}, bf16[128,2,256]{2,1,0:T(2,128)(2,1)S(1)}, bf16[128,2,256]{2,1,0:T(2,128)(2,1)S(1)}, bf16[128,2,256]{2,1,0:T(2,128)(2,1)S(1)}) fusion(bf16[128,2,2,256]{3,2,1,0:T(2,128)(2,1)S(1)} %reshape.277, s32[]{:T(128)S(6)} %select_n.514, s32[]{:T(128)S(6)} %select_n.515, ...), kind=kLoop, calls=%fused_computation.84 | loop fusion | bytes 1048584 | tf_op jit(solution)/shard_map/jit(dynamic_index_in_dim)/dynamic_slice | solution.py:40
  20.3 3.6 %dynamic-slice_reduce_fusion.1 = (bf16[128,2,512]{2,1,0:T(2,128)(2,1)S(1)}, bf16[128,2,512]{2,1,0:T(2,128)(2,1)S(1)}) fusion(bf16[128,2,2,512]{3,2,1,0:T(2,128)(2,1)S(1)} %reshape.272, s32[]{:T(128)S(6)} %select_n.514, s32[]{:T(128)S(6)} %select_n.515), kind=kLoop, calls=%fused_computation.64 | loop fusion | bytes 1048584 | tf_op jit(solution)/shard_map/jit(dynamic_index_in_dim)/dynamic_slice | solution.py:40
  28.4 5.0 %collective-permute-start.3 = (s32[256]{0:T(256)S(1)}, s32[256]{0:T(256)}, u32[]{:S(2)}, u32[]{:S(2)}) collective-permute-start(s32[256]{0:T(256)S(1)} %add_add_fusion), channel_id=1, source_target_pairs={{0,2},{1,3},{4,6},{5,7},{8,10},{9,11},{12,14},{13,15},{16,18},{17,... | collective-permute-start | bytes 3080 | tf_op jit(solution)/shard_map/ppermute | solution.py:219
  34.2 2.2 collective-permute-start.4
  37.3 6.8 %collective-permute-done.4 = bf16[72,512]{1,0:T(8,128)(2,1)S(1)} collective-permute-done((bf16[72,512]{1,0:T(8,128)(2,1)}, bf16[72,512]{1,0:T(8,128)(2,1)S(1)}, u32[]{:S(2)}, u32[]{:S(2)}) %collective-permute-start.4) | collective-permute-done | bytes 73760 | tf_op jit(solution)/shard_map/ppermute | solution.py:32
  44.1 2.0 collective-permute-start.5
  46.1 2.3 collective-permute-done.5
  48.5 2.1 collective-permute-start.10
  55.1 1.6 collective-permute-done.10
  56.8 3.3 %collective-permute-start.13 = (bf16[4,72,512]{2,1,0:T(8,128)(2,1)S(1)}, bf16[4,72,512]{2,1,0:T(8,128)(2,1)S(1)}, u32[]{:S(2)}, u32[]{:S(2)}) collective-permute-start(bf16[4,72,512]{2,1,0:T(8,128)(2,1)S(1)} %get-tuple-element.53), channel_id=1, source_target_pairs={{0,8},{4,12},{8,0},{12,4},{1,9},{5,13},{9,1},{13,5},{2,10},{6,14},... | collective-permute-start | bytes 884744 | tf_op jit(solution)/shard_map/ppermute | solution.py:23
  65.8 6.2 %collective-permute-done.11 = bf16[4,72,512]{2,1,0:T(8,128)(2,1)S(1)} collective-permute-done((bf16[4,72,512]{2,1,0:T(8,128)(2,1)S(1)}, bf16[4,72,512]{2,1,0:T(8,128)(2,1)S(1)}, u32[]{:S(2)}, u32[]{:S(2)}) %collective-permute-start.11) | collective-permute-done | bytes 294944 | tf_op jit(solution)/shard_map/ppermute | solution.py:23
  72.0 3.0 collective-permute-start.19
  77.2 2.6 collective-permute-start.18
  80.6 6.9 %collective-permute-done.17 = bf16[4,72,512]{2,1,0:T(8,128)(2,1)S(1)} collective-permute-done((bf16[4,72,512]{2,1,0:T(8,128)(2,1)S(1)}, bf16[4,72,512]{2,1,0:T(8,128)(2,1)S(1)}, u32[]{:S(2)}, u32[]{:S(2)}) %collective-permute-start.17) | collective-permute-done | bytes 294944 | tf_op jit(solution)/shard_map/ppermute | solution.py:23
  88.8 1.5 collective-permute-start.14
  91.7 4.5 %collective-permute-start.22 = (bf16[4,4,72,512]{3,2,1,0:T(8,128)(2,1)}, bf16[4,4,72,512]{3,2,1,0:T(8,128)(2,1)}, u32[]{:S(2)}, u32[]{:S(2)}) collective-permute-start(bf16[4,4,72,512]{3,2,1,0:T(8,128)(2,1)} %bitcast_dynamic-update-slice_fusion.8), channel_id=1, source_target_pairs={{0,8},{4,12},{8,0},{12,4},{1,9},{5,13},{9,1},{13,5},{2,10},{6,14},... | collective-permute-start | bytes 3538952 | tf_op jit(solution)/shard_map/ppermute | solution.py:23
  96.7 1.4 bitcast_dynamic-update-slice_fusion.3
  98.3 5.7 %collective-permute-start.1 = (bf16[256,1024]{1,0:T(8,128)(2,1)S(1)}, bf16[256,1024]{1,0:T(8,128)(2,1)S(1)}, u32[]{:S(2)}, u32[]{:S(2)}) collective-permute-start(bf16[256,1024]{1,0:T(8,128)(2,1)S(1)} %pad_maximum_fusion.2), channel_id=1, source_target_pairs={{0,2},{1,3},{4,6},{5,7},{8,10},{9,11},{12,14},{13,15},{16,18},{17,... | collective-permute-start | bytes 1572872 | tf_op jit(solution)/shard_map/ppermute | solution.py:220
  104.6 1.4 bitcast_dynamic-update-slice_fusion.6
  106.1 8.4 %collective-permute-done.1 = bf16[256,1024]{1,0:T(8,128)(2,1)S(1)} collective-permute-done((bf16[256,1024]{1,0:T(8,128)(2,1)S(1)}, bf16[256,1024]{1,0:T(8,128)(2,1)S(1)}, u32[]{:S(2)}, u32[]{:S(2)}) %collective-permute-start.1) | collective-permute-done | bytes 524320 | tf_op jit(solution)/shard_map/ppermute | solution.py:220
  114.6 4.2 %attend.1 = (bf16[256,1024]{1,0:T(8,128)(2,1)S(1)}, bf16[8,256,512]{2,1,0:T(8,128)(2,1)S(1)}, f32[8,256,512]{2,1,0:T(8,128)S(1)}) custom-call(bf16[256,1024]{1,0:T(8,128)(2,1)S(1)} %pad_maximum_fusion.1.q_ref, bf16[256,512]{1,0:T(8,128)(2,1)S(1)} %get-tuple-element.58.ko_ref, bf16[256,512]{1,0:T(8,128)(2,1)S(1)} %get-tuple-element.56.kx_ref, ...), custom_call_target="tpu_custom_call" | custom-call | flops 536870912 | bytes 9437184 | tf_op jit(solution)/shard_map/attend/pallas_call | solution.py:105
  118.8 2.5 collective-permute-start.20
  121.4 1.4 convolution_convert_fusion.1
  122.8 1.4 convolution_convert_fusion
  124.2 1.5 constant_dynamic-slice_fusion.3
  128.1 19.7 %collective-permute-done.20 = bf16[4,4,72,512]{3,2,1,0:T(8,128)(2,1)} collective-permute-done((bf16[4,4,72,512]{3,2,1,0:T(8,128)(2,1)}, bf16[4,4,72,512]{3,2,1,0:T(8,128)(2,1)}, u32[]{:S(2)}, u32[]{:S(2)}) %collective-permute-start.20) | collective-permute-done | bytes 1179680 | tf_op jit(solution)/shard_map/ppermute | solution.py:23
  147.8 2.8 collective-permute-start.16
  150.6 1.4 bitcast_dynamic-update-slice_fusion.2
  152.0 1.4 collective-permute-start.34
  153.4 1.4 bitcast_dynamic-update-slice_fusion.1
  154.9 2.0 collective-permute-start.35
  156.8 1.4 bitcast_dynamic-update-slice_fusion
  158.3 1.7 collective-permute-start.36
  160.0 1.4 bitcast_dynamic-update-slice_fusion.5
  161.4 1.4 bitcast_dynamic-update-slice_fusion.4
  162.8 1.4 convolution_convert_fusion.2
  164.2 11.4 %collective-permute-done.16 = bf16[4,4,72,512]{3,2,1,0:T(8,128)(2,1)S(1)} collective-permute-done((bf16[4,4,72,512]{3,2,1,0:T(8,128)(2,1)}, bf16[4,4,72,512]{3,2,1,0:T(8,128)(2,1)S(1)}, u32[]{:S(2)}, u32[]{:S(2)}) %collective-permute-start.16) | collective-permute-done | bytes 1179680 | tf_op jit(solution)/shard_map/ppermute | solution.py:23
  175.7 1.4 convolution_convert_fusion.3
  177.2 5.3 %attend_back.1 = (bf16[256,1024]{1,0:T(8,128)(2,1)S(1)}, f32[256,512]{1,0:T(8,128)S(1)}, bf16[256,512]{1,0:T(8,128)(2,1)S(1)}, f32[256,512]{1,0:T(8,128)S(1)}, bf16[256,512]{1,0:T(8,128)(2,1)S(1)}) custom-call(bf16[256,1024]{1,0:T(8,128)(2,1)S(1)} %pad_maximum_fusion.1.q_ref, bf16[256,512]{1,0:T(8,128)(2,1)S(1)} %get-tuple-element.58.ko_ref, ...), custom_call_target="tpu_custom_call" | custom-call | flops 1073741824 | bytes 11534336 | tf_op jit(solution)/shard_map/attend_back/pallas_call | solution.py:125
  183.8 1.9 dynamic-slice_bitcast_fusion.2
  185.8 1.4 fusion.17
  187.2 12.3 %collective-permute-done.26 = bf16[256,1024]{1,0:T(8,128)(2,1)S(1)} collective-permute-done((bf16[256,1024]{1,0:T(8,128)(2,1)S(1)}, bf16[256,1024]{1,0:T(8,128)(2,1)S(1)}, u32[]{:S(2)}, u32[]{:S(2)}) %collective-permute-start.26) | collective-permute-done | bytes 524320 | tf_op jit(solution)/shard_map/ppermute | solution.py:244
  200.0 1.4 convolution_add_fusion
  203.7 1.9 collective-permute-start.30
  205.6 2.4 collective-permute-start.29
  213.2 2.6 fusion.3
  216.6 41.7 %collective-permute-done.28 = bf16[4,288,512]{2,1,0:T(8,128)(2,1)} collective-permute-done((bf16[4,288,512]{2,1,0:T(8,128)(2,1)}, bf16[4,288,512]{2,1,0:T(8,128)(2,1)}, u32[]{:S(2)}, u32[]{:S(2)}) %collective-permute-start.28) | collective-permute-done | bytes 1179680 | tf_op jit(solution)/shard_map/ppermute | solution.py:23
  258.3 1.5 collective-permute-start.39
  259.8 3.0 fusion.6
  263.8 2.0 collective-permute-start.31
  265.7 4.7 %collective-permute-done.37 = bf16[4,72,512]{2,1,0:T(8,128)(2,1)S(1)} collective-permute-done((bf16[4,72,512]{2,1,0:T(8,128)(2,1)S(1)}, bf16[4,72,512]{2,1,0:T(8,128)(2,1)S(1)}, u32[]{:S(2)}, u32[]{:S(2)}) %collective-permute-start.37) | collective-permute-done | bytes 294944 | tf_op jit(solution)/shard_map/ppermute | solution.py:23
  270.4 5.1 %collective-permute-start.33 = (bf16[4,72,512]{2,1,0:T(8,128)(2,1)}, bf16[4,72,512]{2,1,0:T(8,128)(2,1)}, u32[]{:S(2)}, u32[]{:S(2)}) collective-permute-start(bf16[4,72,512]{2,1,0:T(8,128)(2,1)} %get-tuple-element.35), channel_id=1, source_target_pairs={{0,8},{4,12},{8,0},{12,4},{1,9},{5,13},{9,1},{13,5},{2,10},{6,14},... | collective-permute-start | bytes 884744 | tf_op jit(solution)/shard_map/ppermute | solution.py:23
  278.0 1.8 reshape.285
  279.8 2.1 copy.49
  281.9 1.8 reshape.284
  285.0 1.3 fusion.14
  286.4 6.7 %collective-permute-start.44 = (bf16[72,512]{1,0:T(8,128)(2,1)S(1)}, bf16[72,512]{1,0:T(8,128)(2,1)S(1)}, u32[]{:S(2)}, u32[]{:S(2)}) collective-permute-start(bf16[72,512]{1,0:T(8,128)(2,1)S(1)} %get-tuple-element.50), channel_id=1, source_target_pairs={{0,192},{64,2},{128,66},{192,130},{2,194},{66,0},{130,64},{194,128... | collective-permute-start | bytes 221192 | tf_op jit(solution)/shard_map/ppermute | solution.py:32
  293.1 8.3 %collective-permute-start.45 = (bf16[72,512]{1,0:T(8,128)(2,1)S(1)}, bf16[72,512]{1,0:T(8,128)(2,1)S(1)}, u32[]{:S(2)}, u32[]{:S(2)}) collective-permute-start(bf16[72,512]{1,0:T(8,128)(2,1)S(1)} %get-tuple-element.51), channel_id=1, source_target_pairs={{0,66},{64,130},{128,194},{192,0},{2,64},{66,128},{130,192},{194,2... | collective-permute-start | bytes 221192 | tf_op jit(solution)/shard_map/ppermute | solution.py:32
  301.4 6.3 %collective-permute-start.46 = (bf16[72,512]{1,0:T(8,128)(2,1)S(1)}, bf16[72,512]{1,0:T(8,128)(2,1)S(1)}, u32[]{:S(2)}, u32[]{:S(2)}) collective-permute-start(bf16[72,512]{1,0:T(8,128)(2,1)S(1)} %get-tuple-element.52), channel_id=1, source_target_pairs={{0,2},{64,66},{128,130},{192,194},{2,0},{66,64},{130,128},{194,192... | collective-permute-start | bytes 221192 | tf_op jit(solution)/shard_map/ppermute | solution.py:32
  308.5 2.8 collective-permute-start.41
  311.4 4.0 %collective-permute-start.43 = (bf16[72,512]{1,0:T(8,128)(2,1)S(1)}, bf16[72,512]{1,0:T(8,128)(2,1)S(1)}, u32[]{:S(2)}, u32[]{:S(2)}) collective-permute-start(bf16[72,512]{1,0:T(8,128)(2,1)S(1)} %get-tuple-element.49), channel_id=1, source_target_pairs={{0,130},{64,194},{128,0},{192,64},{2,128},{66,192},{130,2},{194,66... | collective-permute-start | bytes 221192 | tf_op jit(solution)/shard_map/ppermute | solution.py:32
  315.4 2.9 fusion
  (156 shorter events, 47.7 us)
Async XLA Ops:
  0.6 53.6 %collective-permute-start.9 = (bf16[72,512]{1,0:T(8,128)(2,1)}, bf16[72,512]{1,0:T(8,128)(2,1)}, u32[]{:S(2)}, u32[]{:S(2)}) collective-permute-start(bf16[72,512]{1,0:T(8,128)(2,1)} %bitcast.195), channel_id=1, source_target_pairs={{0,66},{64,130},{128,194},{192,0},{2,64},{66,128},{130,192},{194,2... | collective-permute-start | bytes 221192 | tf_op jit(solution)/shard_map/ppermute | solution.py:32
  5.7 47.6 %collective-permute-start.8 = (bf16[72,512]{1,0:T(8,128)(2,1)}, bf16[72,512]{1,0:T(8,128)(2,1)}, u32[]{:S(2)}, u32[]{:S(2)}) collective-permute-start(bf16[72,512]{1,0:T(8,128)(2,1)} %bitcast.196), channel_id=1, source_target_pairs={{0,192},{64,2},{128,66},{192,130},{2,194},{66,0},{130,64},{194,128... | collective-permute-start | bytes 221192 | tf_op jit(solution)/shard_map/ppermute | solution.py:32
  5.7 46.1 %collective-permute-start.7 = (bf16[72,512]{1,0:T(8,128)(2,1)}, bf16[72,512]{1,0:T(8,128)(2,1)}, u32[]{:S(2)}, u32[]{:S(2)}) collective-permute-start(bf16[72,512]{1,0:T(8,128)(2,1)} %bitcast.197), channel_id=1, source_target_pairs={{0,130},{64,194},{128,0},{192,64},{2,128},{66,192},{130,2},{194,66... | collective-permute-start | bytes 221192 | tf_op jit(solution)/shard_map/ppermute | solution.py:32
  10.3 40.3 %collective-permute-start.6 = (bf16[72,512]{1,0:T(8,128)(2,1)}, bf16[72,512]{1,0:T(8,128)(2,1)}, u32[]{:S(2)}, u32[]{:S(2)}) collective-permute-start(bf16[72,512]{1,0:T(8,128)(2,1)} %bitcast.198), channel_id=1, source_target_pairs={{0,128},{64,192},{128,2},{192,66},{2,130},{66,194},{130,0},{194,64... | collective-permute-start | bytes 221192 | tf_op jit(solution)/shard_map/ppermute | solution.py:32
  10.3 17.4 %collective-permute-start.2 = (s32[128]{0:T(128)}, s32[128]{0:T(128)}, u32[]{:S(2)}, u32[]{:S(2)}) collective-permute-start(s32[128]{0:T(128)} %param.9), channel_id=1, source_target_pairs={{0,1},{1,0},{2,3},{3,2},{4,5},{5,4},{6,7},{7,6},{8,9},{9,8},{10,11... | collective-permute-start | bytes 1544 | tf_op jit(solution)/shard_map/ppermute | solution.py:36
  10.7 9.3 %copy-start.5 = (bf16[128,2048]{1,0:T(8,128)(2,1)S(1)}, bf16[128,2048]{1,0:T(8,128)(2,1)}, u32[]{:S(2)}) copy-start(bf16[128,2048]{1,0:T(8,128)(2,1)} %param.6) | copy-start | bytes 1572868
  17.3 8.2 %copy-start.3 = (bf16[128,4608]{1,0:T(8,128)(2,1)S(1)}, bf16[128,4608]{1,0:T(8,128)(2,1)}, u32[]{:S(2)}) copy-start(bf16[128,4608]{1,0:T(8,128)(2,1)} %param.11) | copy-start | bytes 3538948
  25.5 18.6 %copy-start.12 = (bf16[512,72]{0,1:T(8,128)(2,1)S(1)}, bf16[512,72]{0,1:T(8,128)(2,1)}, u32[]{:S(2)}) copy-start(bf16[512,72]{0,1:T(8,128)(2,1)} %param.10) | copy-start | bytes 221188
  28.4 5.8 %collective-permute-start.3 = (s32[256]{0:T(256)S(1)}, s32[256]{0:T(256)}, u32[]{:S(2)}, u32[]{:S(2)}) collective-permute-start(s32[256]{0:T(256)S(1)} %add_add_fusion), channel_id=1, source_target_pairs={{0,2},{1,3},{4,6},{5,7},{8,10},{9,11},{12,14},{13,15},{16,18},{17,... | collective-permute-start | bytes 3080 | tf_op jit(solution)/shard_map/ppermute | solution.py:219
  34.2 9.9 %collective-permute-start.4 = (bf16[72,512]{1,0:T(8,128)(2,1)}, bf16[72,512]{1,0:T(8,128)(2,1)S(1)}, u32[]{:S(2)}, u32[]{:S(2)}) collective-permute-start(bf16[72,512]{1,0:T(8,128)(2,1)} %bitcast.199), channel_id=1, source_target_pairs={{0,64},{64,128},{128,192},{192,2},{2,66},{66,130},{130,194},{194,0... | collective-permute-start | bytes 221192 | tf_op jit(solution)/shard_map/ppermute | solution.py:32
  44.1 4.4 %collective-permute-start.5 = (bf16[72,512]{1,0:T(8,128)(2,1)S(1)}, bf16[72,512]{1,0:T(8,128)(2,1)S(1)}, u32[]{:S(2)}, u32[]{:S(2)}) collective-permute-start(bf16[72,512]{1,0:T(8,128)(2,1)S(1)} %bitcast.200), channel_id=1, source_target_pairs={{0,194},{64,0},{128,64},{192,128},{2,192},{66,2},{130,66},{194,130... | collective-permute-start | bytes 221192 | tf_op jit(solution)/shard_map/ppermute | solution.py:32
  48.5 8.3 %collective-permute-start.10 = (bf16[72,512]{1,0:T(8,128)(2,1)S(1)}, bf16[72,512]{1,0:T(8,128)(2,1)S(1)}, u32[]{:S(2)}, u32[]{:S(2)}) collective-permute-start(bf16[72,512]{1,0:T(8,128)(2,1)S(1)} %bitcast.201), channel_id=1, source_target_pairs={{0,2},{64,66},{128,130},{192,194},{2,0},{66,64},{130,128},{194,192... | collective-permute-start | bytes 221192 | tf_op jit(solution)/shard_map/ppermute | solution.py:32
  50.6 68.2 %collective-permute-start.24 = (bf16[128,4608]{1,0:T(8,128)(2,1)}, bf16[128,4608]{1,0:T(8,128)(2,1)S(1)}, u32[]{:S(2)}, u32[]{:S(2)}) collective-permute-start(bf16[128,4608]{1,0:T(8,128)(2,1)} %param.11), channel_id=1, source_target_pairs={{0,1},{1,0},{2,3},{3,2},{4,5},{5,4},{6,7},{7,6},{8,9},{9,8},{10,11... | collective-permute-start | bytes 3538952 | tf_op jit(solution)/shard_map/ppermute | solution.py:36
  51.8 46.4 %collective-permute-start = (bf16[128,2048]{1,0:T(8,128)(2,1)S(1)}, bf16[128,2048]{1,0:T(8,128)(2,1)S(1)}, u32[]{:S(2)}, u32[]{:S(2)}) collective-permute-start(bf16[128,2048]{1,0:T(8,128)(2,1)S(1)} %pad_maximum_fusion), channel_id=1, source_target_pairs={{0,1},{1,0},{2,3},{3,2},{4,5},{5,4},{6,7},{7,6},{8,9},{9,8},{10,11... | collective-permute-start | bytes 1572872 | tf_op jit(solution)/shard_map/ppermute | solution.py:36
  56.8 20.4 %collective-permute-start.13 = (bf16[4,72,512]{2,1,0:T(8,128)(2,1)S(1)}, bf16[4,72,512]{2,1,0:T(8,128)(2,1)S(1)}, u32[]{:S(2)}, u32[]{:S(2)}) collective-permute-start(bf16[4,72,512]{2,1,0:T(8,128)(2,1)S(1)} %get-tuple-element.53), channel_id=1, source_target_pairs={{0,8},{4,12},{8,0},{12,4},{1,9},{5,13},{9,1},{13,5},{2,10},{6,14},... | collective-permute-start | bytes 884744 | tf_op jit(solution)/shard_map/ppermute | solution.py:23
  60.1 15.8 %collective-permute-start.12 = (bf16[4,72,512]{2,1,0:T(8,128)(2,1)S(1)}, bf16[4,72,512]{2,1,0:T(8,128)(2,1)S(1)}, u32[]{:S(2)}, u32[]{:S(2)}) collective-permute-start(bf16[4,72,512]{2,1,0:T(8,128)(2,1)S(1)} %get-tuple-element.53), channel_id=1, source_target_pairs={{0,12},{4,0},{8,4},{12,8},{1,13},{5,1},{9,5},{13,9},{2,14},{6,2},{... | collective-permute-start | bytes 884744 | tf_op jit(solution)/shard_map/ppermute | solution.py:23
  61.1 10.9 %collective-permute-start.11 = (bf16[4,72,512]{2,1,0:T(8,128)(2,1)S(1)}, bf16[4,72,512]{2,1,0:T(8,128)(2,1)S(1)}, u32[]{:S(2)}, u32[]{:S(2)}) collective-permute-start(bf16[4,72,512]{2,1,0:T(8,128)(2,1)S(1)} %get-tuple-element.53), channel_id=1, source_target_pairs={{0,4},{4,8},{8,12},{12,0},{1,5},{5,9},{9,13},{13,1},{2,6},{6,10},{... | collective-permute-start | bytes 884744 | tf_op jit(solution)/shard_map/ppermute | solution.py:23
  72.0 18.9 %collective-permute-start.19 = (bf16[4,72,512]{2,1,0:T(8,128)(2,1)S(1)}, bf16[4,72,512]{2,1,0:T(8,128)(2,1)S(1)}, u32[]{:S(2)}, u32[]{:S(2)}) collective-permute-start(bf16[4,72,512]{2,1,0:T(8,128)(2,1)S(1)} %get-tuple-element.54), channel_id=1, source_target_pairs={{0,32},{16,48},{32,0},{48,16},{1,33},{17,49},{33,1},{49,17},{2,34}... | collective-permute-start | bytes 884744 | tf_op jit(solution)/shard_map/ppermute | solution.py:23
  75.8 11.6 %collective-permute-start.17 = (bf16[4,72,512]{2,1,0:T(8,128)(2,1)S(1)}, bf16[4,72,512]{2,1,0:T(8,128)(2,1)S(1)}, u32[]{:S(2)}, u32[]{:S(2)}) collective-permute-start(bf16[4,72,512]{2,1,0:T(8,128)(2,1)S(1)} %get-tuple-element.54), channel_id=1, source_target_pairs={{0,16},{16,32},{32,48},{48,0},{1,17},{17,33},{33,49},{49,1},{2,18}... | collective-permute-start | bytes 884744 | tf_op jit(solution)/shard_map/ppermute | solution.py:23
  77.2 11.6 %collective-permute-start.18 = (bf16[4,72,512]{2,1,0:T(8,128)(2,1)S(1)}, bf16[4,72,512]{2,1,0:T(8,128)(2,1)S(1)}, u32[]{:S(2)}, u32[]{:S(2)}) collective-permute-start(bf16[4,72,512]{2,1,0:T(8,128)(2,1)S(1)} %get-tuple-element.54), channel_id=1, source_target_pairs={{0,48},{16,0},{32,16},{48,32},{1,49},{17,1},{33,17},{49,33},{2,50}... | collective-permute-start | bytes 884744 | tf_op jit(solution)/shard_map/ppermute | solution.py:23
  87.5 73.9 %collective-permute-start.15 = (bf16[4,4,72,512]{3,2,1,0:T(8,128)(2,1)}, bf16[4,4,72,512]{3,2,1,0:T(8,128)(2,1)}, u32[]{:S(2)}, u32[]{:S(2)}) collective-permute-start(bf16[4,4,72,512]{3,2,1,0:T(8,128)(2,1)} %bitcast_dynamic-update-slice_fusion.15), channel_id=1, source_target_pairs={{0,48},{16,0},{32,16},{48,32},{1,49},{17,1},{33,17},{49,33},{2,50}... | collective-permute-start | bytes 3538952 | tf_op jit(solution)/shard_map/ppermute | solution.py:23
  88.8 69.5 %collective-permute-start.14 = (bf16[4,4,72,512]{3,2,1,0:T(8,128)(2,1)}, bf16[4,4,72,512]{3,2,1,0:T(8,128)(2,1)}, u32[]{:S(2)}, u32[]{:S(2)}) collective-permute-start(bf16[4,4,72,512]{3,2,1,0:T(8,128)(2,1)} %bitcast_dynamic-update-slice_fusion.15), channel_id=1, source_target_pairs={{0,16},{16,32},{32,48},{48,0},{1,17},{17,33},{33,49},{49,1},{2,18}... | collective-permute-start | bytes 3538952 | tf_op jit(solution)/shard_map/ppermute | solution.py:23
  91.7 63.2 %collective-permute-start.22 = (bf16[4,4,72,512]{3,2,1,0:T(8,128)(2,1)}, bf16[4,4,72,512]{3,2,1,0:T(8,128)(2,1)}, u32[]{:S(2)}, u32[]{:S(2)}) collective-permute-start(bf16[4,4,72,512]{3,2,1,0:T(8,128)(2,1)} %bitcast_dynamic-update-slice_fusion.8), channel_id=1, source_target_pairs={{0,8},{4,12},{8,0},{12,4},{1,9},{5,13},{9,1},{13,5},{2,10},{6,14},... | collective-permute-start | bytes 3538952 | tf_op jit(solution)/shard_map/ppermute | solution.py:23
  96.7 1.5 copy-start.8
  96.7 1.5 copy-start.9
  98.3 16.2 %collective-permute-start.1 = (bf16[256,1024]{1,0:T(8,128)(2,1)S(1)}, bf16[256,1024]{1,0:T(8,128)(2,1)S(1)}, u32[]{:S(2)}, u32[]{:S(2)}) collective-permute-start(bf16[256,1024]{1,0:T(8,128)(2,1)S(1)} %pad_maximum_fusion.2), channel_id=1, source_target_pairs={{0,2},{1,3},{4,6},{5,7},{8,10},{9,11},{12,14},{13,15},{16,18},{17,... | collective-permute-start | bytes 1572872 | tf_op jit(solution)/shard_map/ppermute | solution.py:220
  104.5 1.5 copy-start.4
  114.5 37.5 %collective-permute-start.21 = (bf16[4,4,72,512]{3,2,1,0:T(8,128)(2,1)}, bf16[4,4,72,512]{3,2,1,0:T(8,128)(2,1)}, u32[]{:S(2)}, u32[]{:S(2)}) collective-permute-start(bf16[4,4,72,512]{3,2,1,0:T(8,128)(2,1)} %bitcast_dynamic-update-slice_fusion.8), channel_id=1, source_target_pairs={{0,12},{4,0},{8,4},{12,8},{1,13},{5,1},{9,5},{13,9},{2,14},{6,2},{... | collective-permute-start | bytes 3538952 | tf_op jit(solution)/shard_map/ppermute | solution.py:23
  118.8 29.0 %collective-permute-start.20 = (bf16[4,4,72,512]{3,2,1,0:T(8,128)(2,1)}, bf16[4,4,72,512]{3,2,1,0:T(8,128)(2,1)}, u32[]{:S(2)}, u32[]{:S(2)}) collective-permute-start(bf16[4,4,72,512]{3,2,1,0:T(8,128)(2,1)} %bitcast_dynamic-update-slice_fusion.8), channel_id=1, source_target_pairs={{0,4},{4,8},{8,12},{12,0},{1,5},{5,9},{9,13},{13,1},{2,6},{6,10},{... | collective-permute-start | bytes 3538952 | tf_op jit(solution)/shard_map/ppermute | solution.py:23
  122.8 61.0 %copy-start = (bf16[4608,512]{1,0:T(8,128)(2,1)}, bf16[4608,512]{1,0:T(8,128)(2,1)S(1)}, u32[]{:S(2)}) copy-start(bf16[4608,512]{1,0:T(8,128)(2,1)S(1)} %convolution_convert_fusion.1) | copy-start | bytes 14155780
  147.8 27.8 %collective-permute-start.16 = (bf16[4,4,72,512]{3,2,1,0:T(8,128)(2,1)}, bf16[4,4,72,512]{3,2,1,0:T(8,128)(2,1)S(1)}, u32[]{:S(2)}, u32[]{:S(2)}) collective-permute-start(bf16[4,4,72,512]{3,2,1,0:T(8,128)(2,1)} %bitcast_dynamic-update-slice_fusion.15), channel_id=1, source_target_pairs={{0,32},{16,48},{32,0},{48,16},{1,33},{17,49},{33,1},{49,17},{2,34}... | collective-permute-start | bytes 3538952 | tf_op jit(solution)/shard_map/ppermute | solution.py:23
  152.0 53.6 %collective-permute-start.34 = (bf16[4,4,72,512]{3,2,0,1:T(8,128)(2,1)S(1)}, bf16[4,4,72,512]{3,2,0,1:T(8,128)(2,1)}, u32[]{:S(2)}, u32[]{:S(2)}) collective-permute-start(bf16[4,4,72,512]{3,2,0,1:T(8,128)(2,1)S(1)} %bitcast.182), channel_id=1, source_target_pairs={{0,4},{4,8},{8,12},{12,0},{1,5},{5,9},{9,13},{13,1},{2,6},{6,10},{... | collective-permute-start | bytes 3538952 | tf_op jit(solution)/shard_map/ppermute | solution.py:23
  154.9 58.2 %collective-permute-start.35 = (bf16[4,4,72,512]{3,2,0,1:T(8,128)(2,1)}, bf16[4,4,72,512]{3,2,0,1:T(8,128)(2,1)}, u32[]{:S(2)}, u32[]{:S(2)}) collective-permute-start(bf16[4,4,72,512]{3,2,0,1:T(8,128)(2,1)} %bitcast.171), channel_id=1, source_target_pairs={{0,12},{4,0},{8,4},{12,8},{1,13},{5,1},{9,5},{13,9},{2,14},{6,2},{... | collective-permute-start | bytes 3538952 | tf_op jit(solution)/shard_map/ppermute | solution.py:23
  158.3 54.9 %collective-permute-start.36 = (bf16[4,4,72,512]{3,2,0,1:T(8,128)(2,1)}, bf16[4,4,72,512]{3,2,0,1:T(8,128)(2,1)}, u32[]{:S(2)}, u32[]{:S(2)}) collective-permute-start(bf16[4,4,72,512]{3,2,0,1:T(8,128)(2,1)} %bitcast.170), channel_id=1, source_target_pairs={{0,8},{4,12},{8,0},{12,4},{1,9},{5,13},{9,1},{13,5},{2,10},{6,14},... | collective-permute-start | bytes 3538952 | tf_op jit(solution)/shard_map/ppermute | solution.py:23
  182.5 17.0 %collective-permute-start.26 = (bf16[256,1024]{1,0:T(8,128)(2,1)S(1)}, bf16[256,1024]{1,0:T(8,128)(2,1)S(1)}, u32[]{:S(2)}, u32[]{:S(2)}) collective-permute-start(bf16[256,1024]{1,0:T(8,128)(2,1)S(1)} %pad_maximum_fusion.5), channel_id=1, source_target_pairs={{2,0},{3,1},{6,4},{7,5},{10,8},{11,9},{14,12},{15,13},{18,16},{19,... | collective-permute-start | bytes 1572872 | tf_op jit(solution)/shard_map/ppermute | solution.py:244
  185.7 17.0 %collective-permute-start.25 = (bf16[128,1024]{1,0:T(8,128)(2,1)S(1)}, bf16[128,1024]{1,0:T(8,128)(2,1)S(1)}, u32[]{:S(2)}, u32[]{:S(2)}) collective-permute-start(bf16[128,1024]{1,0:T(8,128)(2,1)S(1)} %slice.73), channel_id=1, source_target_pairs={{0,1},{1,0},{2,3},{3,2},{4,5},{5,4},{6,7},{7,6},{8,9},{9,8},{10,11... | collective-permute-start | bytes 786440 | tf_op jit(solution)/shard_map/ppermute | solution.py:36
  199.7 4.0 %collective-permute-start.27 = (bf16[128,1024]{1,0:T(8,128)(2,1)S(1)}, bf16[128,1024]{1,0:T(8,128)(2,1)S(1)}, u32[]{:S(2)}, u32[]{:S(2)}) collective-permute-start(bf16[128,1024]{1,0:T(8,128)(2,1)S(1)} %slice.90), channel_id=1, source_target_pairs={{0,1},{1,0},{2,3},{3,2},{4,5},{5,4},{6,7},{7,6},{8,9},{9,8},{10,11... | collective-permute-start | bytes 786440 | tf_op jit(solution)/shard_map/ppermute | solution.py:36
  201.4 6.7 %copy-start.1 = (f32[256,4608]{1,0:T(8,128)}, f32[256,4608]{1,0:T(8,128)S(1)}, u32[]{:S(2)}) copy-start(f32[256,4608]{1,0:T(8,128)S(1)} %convolution_add_fusion) | copy-start | bytes 14155780
  202.7 55.6 %collective-permute-start.28 = (bf16[4,288,512]{2,1,0:T(8,128)(2,1)}, bf16[4,288,512]{2,1,0:T(8,128)(2,1)}, u32[]{:S(2)}, u32[]{:S(2)}) collective-permute-start(bf16[4,288,512]{2,1,0:T(8,128)(2,1)} %get-tuple-element.27), channel_id=1, source_target_pairs={{0,16},{16,32},{32,48},{48,0},{1,17},{17,33},{33,49},{49,1},{2,18}... | collective-permute-start | bytes 3538952 | tf_op jit(solution)/shard_map/ppermute | solution.py:23
  203.7 56.0 %collective-permute-start.30 = (bf16[4,288,512]{2,1,0:T(8,128)(2,1)}, bf16[4,288,512]{2,1,0:T(8,128)(2,1)}, u32[]{:S(2)}, u32[]{:S(2)}) collective-permute-start(bf16[4,288,512]{2,1,0:T(8,128)(2,1)} %get-tuple-element.28), channel_id=1, source_target_pairs={{0,32},{16,48},{32,0},{48,16},{1,33},{17,49},{33,1},{49,17},{2,34}... | collective-permute-start | bytes 3538952 | tf_op jit(solution)/shard_map/ppermute | solution.py:23
  205.6 54.1 %collective-permute-start.29 = (bf16[4,288,512]{2,1,0:T(8,128)(2,1)}, bf16[4,288,512]{2,1,0:T(8,128)(2,1)}, u32[]{:S(2)}, u32[]{:S(2)}) collective-permute-start(bf16[4,288,512]{2,1,0:T(8,128)(2,1)} %get-tuple-element.29), channel_id=1, source_target_pairs={{0,48},{16,0},{32,16},{48,32},{1,49},{17,1},{33,17},{49,33},{2,50}... | collective-permute-start | bytes 3538952 | tf_op jit(solution)/shard_map/ppermute | solution.py:23
  209.2 4.0 %copy-start.2 = (bf16[4,4,1,72,512]{4,3,2,1,0:T(8,128)(2,1)S(1)}, bf16[4,4,1,72,512]{4,3,2,1,0:T(8,128)(2,1)}, u32[]{:S(2)}) copy-start(bf16[4,4,1,72,512]{4,3,2,1,0:T(8,128)(2,1)} %get-tuple-element.30) | copy-start | bytes 3538948
  213.1 95.4 %collective-permute-start.23 = (bf16[128,4608]{1,0:T(8,128)(2,1)}, bf16[128,4608]{1,0:T(8,128)(2,1)S(1)}, u32[]{:S(2)}, u32[]{:S(2)}) collective-permute-start(bf16[128,4608]{1,0:T(8,128)(2,1)} %slice.120), channel_id=1, source_target_pairs={{0,1},{1,0},{2,3},{3,2},{4,5},{5,4},{6,7},{7,6},{8,9},{9,8},{10,11... | collective-permute-start | bytes 3538952 | tf_op jit(solution)/shard_map/ppermute | solution.py:36
  216.6 53.8 %collective-permute-start.37 = (bf16[4,72,512]{2,1,0:T(8,128)(2,1)S(1)}, bf16[4,72,512]{2,1,0:T(8,128)(2,1)S(1)}, u32[]{:S(2)}, u32[]{:S(2)}) collective-permute-start(bf16[4,72,512]{2,1,0:T(8,128)(2,1)S(1)} %get-tuple-element.37), channel_id=1, source_target_pairs={{0,16},{16,32},{32,48},{48,0},{1,17},{17,33},{33,49},{49,1},{2,18}... | collective-permute-start | bytes 884744 | tf_op jit(solution)/shard_map/ppermute | solution.py:23
  258.3 17.3 %collective-permute-start.39 = (bf16[4,72,512]{2,1,0:T(8,128)(2,1)S(1)}, bf16[4,72,512]{2,1,0:T(8,128)(2,1)S(1)}, u32[]{:S(2)}, u32[]{:S(2)}) collective-permute-start(bf16[4,72,512]{2,1,0:T(8,128)(2,1)S(1)} %get-tuple-element.38), channel_id=1, source_target_pairs={{0,32},{16,48},{32,0},{48,16},{1,33},{17,49},{33,1},{49,17},{2,34}... | collective-permute-start | bytes 884744 | tf_op jit(solution)/shard_map/ppermute | solution.py:23
  259.7 16.0 %copy-start.6 = (bf16[128,2,1,256]{3,1,0,2:T(2,128)(2,1)S(1)}, bf16[128,2,1,256]{3,1,0,2:T(2,128)(2,1)}, u32[]{:S(2)}) copy-start(bf16[128,2,1,256]{3,1,0,2:T(2,128)(2,1)} %select_n.579) | copy-start | bytes 393220
  259.7 16.0 %copy-start.7 = (bf16[128,2,1,256]{3,1,0,2:T(2,128)(2,1)S(1)}, bf16[128,2,1,256]{3,1,0,2:T(2,128)(2,1)}, u32[]{:S(2)}) copy-start(bf16[128,2,1,256]{3,1,0,2:T(2,128)(2,1)} %select_n.577) | copy-start | bytes 393220
  259.7 24.0 %collective-permute-start.38 = (bf16[4,72,512]{2,1,0:T(8,128)(2,1)}, bf16[4,72,512]{2,1,0:T(8,128)(2,1)}, u32[]{:S(2)}, u32[]{:S(2)}) collective-permute-start(bf16[4,72,512]{2,1,0:T(8,128)(2,1)} %get-tuple-element.39), channel_id=1, source_target_pairs={{0,48},{16,0},{32,16},{48,32},{1,49},{17,1},{33,17},{49,33},{2,50}... | collective-permute-start | bytes 884744 | tf_op jit(solution)/shard_map/ppermute | solution.py:23
  263.8 21.2 %collective-permute-start.31 = (bf16[4,72,512]{2,1,0:T(8,128)(2,1)}, bf16[4,72,512]{2,1,0:T(8,128)(2,1)}, u32[]{:S(2)}, u32[]{:S(2)}) collective-permute-start(bf16[4,72,512]{2,1,0:T(8,128)(2,1)} %get-tuple-element.34), channel_id=1, source_target_pairs={{0,4},{4,8},{8,12},{12,0},{1,5},{5,9},{9,13},{13,1},{2,6},{6,10},{... | collective-permute-start | bytes 884744 | tf_op jit(solution)/shard_map/ppermute | solution.py:23
  270.4 6.4 %copy-start.10 = (bf16[4,72,512]{2,1,0:T(8,128)(2,1)}, bf16[4,72,512]{2,1,0:T(8,128)(2,1)S(1)}, u32[]{:S(2)}) copy-start(bf16[4,72,512]{2,1,0:T(8,128)(2,1)S(1)} %collective-permute-done.37) | copy-start | bytes 884740
  270.4 14.6 %collective-permute-start.33 = (bf16[4,72,512]{2,1,0:T(8,128)(2,1)}, bf16[4,72,512]{2,1,0:T(8,128)(2,1)}, u32[]{:S(2)}, u32[]{:S(2)}) collective-permute-start(bf16[4,72,512]{2,1,0:T(8,128)(2,1)} %get-tuple-element.35), channel_id=1, source_target_pairs={{0,8},{4,12},{8,0},{12,4},{1,9},{5,13},{9,1},{13,5},{2,10},{6,14},... | collective-permute-start | bytes 884744 | tf_op jit(solution)/shard_map/ppermute | solution.py:23
  275.5 1.3 copy-start.11
  275.5 9.5 %collective-permute-start.32 = (bf16[4,72,512]{2,1,0:T(8,128)(2,1)}, bf16[4,72,512]{2,1,0:T(8,128)(2,1)}, u32[]{:S(2)}, u32[]{:S(2)}) collective-permute-start(bf16[4,72,512]{2,1,0:T(8,128)(2,1)} %get-tuple-element.36), channel_id=1, source_target_pairs={{0,12},{4,0},{8,4},{12,8},{1,13},{5,1},{9,5},{13,9},{2,14},{6,2},{... | collective-permute-start | bytes 884744 | tf_op jit(solution)/shard_map/ppermute | solution.py:23
  286.4 24.8 %collective-permute-start.44 = (bf16[72,512]{1,0:T(8,128)(2,1)S(1)}, bf16[72,512]{1,0:T(8,128)(2,1)S(1)}, u32[]{:S(2)}, u32[]{:S(2)}) collective-permute-start(bf16[72,512]{1,0:T(8,128)(2,1)S(1)} %get-tuple-element.50), channel_id=1, source_target_pairs={{0,192},{64,2},{128,66},{192,130},{2,194},{66,0},{130,64},{194,128... | collective-permute-start | bytes 221192 | tf_op jit(solution)/shard_map/ppermute | solution.py:32
  293.1 18.3 %collective-permute-start.45 = (bf16[72,512]{1,0:T(8,128)(2,1)S(1)}, bf16[72,512]{1,0:T(8,128)(2,1)S(1)}, u32[]{:S(2)}, u32[]{:S(2)}) collective-permute-start(bf16[72,512]{1,0:T(8,128)(2,1)S(1)} %get-tuple-element.51), channel_id=1, source_target_pairs={{0,66},{64,130},{128,194},{192,0},{2,64},{66,128},{130,192},{194,2... | collective-permute-start | bytes 221192 | tf_op jit(solution)/shard_map/ppermute | solution.py:32
  301.4 16.8 %collective-permute-start.46 = (bf16[72,512]{1,0:T(8,128)(2,1)S(1)}, bf16[72,512]{1,0:T(8,128)(2,1)S(1)}, u32[]{:S(2)}, u32[]{:S(2)}) collective-permute-start(bf16[72,512]{1,0:T(8,128)(2,1)S(1)} %get-tuple-element.52), channel_id=1, source_target_pairs={{0,2},{64,66},{128,130},{192,194},{2,0},{66,64},{130,128},{194,192... | collective-permute-start | bytes 221192 | tf_op jit(solution)/shard_map/ppermute | solution.py:32
  307.9 10.3 %collective-permute-start.40 = (bf16[72,512]{1,0:T(8,128)(2,1)S(1)}, bf16[72,512]{1,0:T(8,128)(2,1)S(1)}, u32[]{:S(2)}, u32[]{:S(2)}) collective-permute-start(bf16[72,512]{1,0:T(8,128)(2,1)S(1)} %get-tuple-element.46), channel_id=1, source_target_pairs={{0,64},{64,128},{128,192},{192,2},{2,66},{66,130},{130,194},{194,0... | collective-permute-start | bytes 221192 | tf_op jit(solution)/shard_map/ppermute | solution.py:32
  308.5 9.8 %collective-permute-start.41 = (bf16[72,512]{1,0:T(8,128)(2,1)S(1)}, bf16[72,512]{1,0:T(8,128)(2,1)S(1)}, u32[]{:S(2)}, u32[]{:S(2)}) collective-permute-start(bf16[72,512]{1,0:T(8,128)(2,1)S(1)} %get-tuple-element.47), channel_id=1, source_target_pairs={{0,194},{64,0},{128,64},{192,128},{2,192},{66,2},{130,66},{194,130... | collective-permute-start | bytes 221192 | tf_op jit(solution)/shard_map/ppermute | solution.py:32
  311.2 7.0 %collective-permute-start.42 = (bf16[72,512]{1,0:T(8,128)(2,1)S(1)}, bf16[72,512]{1,0:T(8,128)(2,1)S(1)}, u32[]{:S(2)}, u32[]{:S(2)}) collective-permute-start(bf16[72,512]{1,0:T(8,128)(2,1)S(1)} %get-tuple-element.48), channel_id=1, source_target_pairs={{0,128},{64,192},{128,2},{192,66},{2,130},{66,194},{130,0},{194,64... | collective-permute-start | bytes 221192 | tf_op jit(solution)/shard_map/ppermute | solution.py:32
  311.4 6.9 %collective-permute-start.43 = (bf16[72,512]{1,0:T(8,128)(2,1)S(1)}, bf16[72,512]{1,0:T(8,128)(2,1)S(1)}, u32[]{:S(2)}, u32[]{:S(2)}) collective-permute-start(bf16[72,512]{1,0:T(8,128)(2,1)S(1)} %get-tuple-element.49), channel_id=1, source_target_pairs={{0,130},{64,194},{128,0},{192,64},{2,128},{66,192},{130,2},{194,66... | collective-permute-start | bytes 221192 | tf_op jit(solution)/shard_map/ppermute | solution.py:32
